TPU v7x, 32 devices: a whole 2x2x4 slice. The times are simulated.
32 devices in a mesh: cin: 8 (over z, x), cout: 2 (over y), depth: 2 (over core).
Axes of the slice: x: 2, y: 2, z: 4, core: 2. Of those that a mesh axis runs over, the one named last changes fastest.
Arguments:
- features: bfloat16 [8, 512, 4, 128], P(None, 'cin', 'depth'), may hold values from -6 to 6
- kernel: bfloat16 [27, 512, 512], P(None, 'cout', 'cin'), may hold values from -0.0546875 to 0.0546875
- grad_out: bfloat16 [8, 512, 4, 128], P('cin', 'cout', 'depth'), may hold values from -6 to 6
Outputs:
- output: bfloat16 [8, 512, 4, 128], P('cin', 'cout', 'depth')
- input_grad: bfloat16 [8, 512, 4, 128], P('cout', 'cin', 'depth')
- kernel_grad: float32 [27, 512, 512], P(None, 'cout', 'cin')
All inputs are finite; a program needn't handle non-finite values.
Results may differ from a plain program's by a relative error of at most 0.001.
Values may be sent and summed in bfloat16 or wider, within the bound.
No kernel may reach another device: no remote copies, remote signals or barrier semaphores. Data moves between devices by JAX's collectives and lax.ppermute only.
A program may use at most 128 MiB of HBM per device.

v0:
```python
import math
import jax
import jax.numpy as jnp
from jax import lax
from jax.sharding import PartitionSpec as P


def padded_2(x, sides, width):
    for axis, dim in sides:
        size, length = (lax.axis_size(axis), x.shape[dim])
        up = [(i, (i + 1) % size) for i in range(size - 1)]
        down = [(j, i) for i, j in up]
        last = lax.slice_in_dim(x, length - width, length, axis=dim)
        first = lax.slice_in_dim(x, 0, width, axis=dim)
        before = lax.ppermute(last, axis, up)
        after = lax.ppermute(first, axis, down)
        x = jnp.concatenate([before, x, after], axis=dim)
    return x


def conv_rows(padded, weight, count, slab, width):
    total = None
    for depth_off in range(3):
        pieces = [
            padded[
                row_off : row_off + count,
                :,
                depth_off : depth_off + slab,
                col_off : col_off + width,
            ]
            for row_off in range(3)
            for col_off in range(3)
        ]
        stacked = jnp.stack(pieces, axis=1)
        term = jnp.einsum(
            "toc,htcdw->hodw",
            weight[9 * depth_off : 9 * depth_off + 9],
            stacked,
            preferred_element_type=jnp.float32,
        )
        total = term if total is None else total + term
    return total


def weight_terms(padded, grad_own, count, slab, width):
    parts = []
    for depth_off in range(3):
        pieces = [
            padded[
                row_off : row_off + count,
                :,
                depth_off : depth_off + slab,
                col_off : col_off + width,
            ]
            for row_off in range(3)
            for col_off in range(3)
        ]
        stacked = jnp.stack(pieces, axis=1)
        parts.append(
            jnp.einsum("hodw,htcdw->toc", grad_own, stacked, preferred_element_type=jnp.float32)
        )
    return jnp.concatenate(parts, axis=0)


def per_device(features, kernel, grad_out):
    rows_all = features.shape[0]
    slab = features.shape[2]
    width = features.shape[3]
    chan_in = features.shape[1]
    rows_own = rows_all // lax.axis_size("cin")
    slab_ext = padded_2(features, (("depth", 2),), 1)
    feat_pad = jnp.pad(slab_ext, ((1, 1), (0, 0), (0, 0), (1, 1)))
    block = feat_pad
    output = lax.psum_scatter(
        conv_rows(block, kernel, lax.axis_size("cin") * rows_own, slab, width),
        "cin",
        scatter_dimension=0,
        tiled=True,
    ).astype(jnp.bfloat16)
    grad_full = lax.all_gather(grad_out, "cin", axis=0, tiled=True)
    grad_full = padded_2(grad_full, (("depth", 2),), 1)
    grad_pad = jnp.pad(grad_full, ((1, 1), (0, 0), (0, 0), (0, 0)))
    rows_grad = rows_all // lax.axis_size("cout")
    block = grad_pad
    total = jnp.zeros((lax.axis_size("cout") * rows_grad, chan_in, slab, width), jnp.float32)
    for depth_off in range(3):
        part = block[:, :, 2 - depth_off : 2 - depth_off + slab, :]
        mixed = jnp.einsum(
            "toc,hodw->thcdw",
            kernel[9 * depth_off : 9 * depth_off + 9],
            part,
            preferred_element_type=jnp.float32,
        )
        mixed = jnp.pad(mixed, ((0, 0), (0, 0), (0, 0), (0, 0), (1, 1)))
        for row_off in range(3):
            for col_off in range(3):
                total = (
                    total
                    + mixed[
                        3 * row_off + col_off,
                        2 - row_off : 2 - row_off + lax.axis_size("cout") * rows_grad,
                        :,
                        :,
                        2 - col_off : 2 - col_off + width,
                    ]
                )
    input_grad = lax.psum_scatter(total, "cout", scatter_dimension=0, tiled=True).astype(
        jnp.bfloat16
    )
    grad_own = grad_full[:, :, 1 : 1 + slab, :]
    local_terms = weight_terms(feat_pad, grad_own, rows_all, slab, width)
    summed = lax.psum(local_terms, "depth")
    cells = rows_all * slab * lax.axis_size("depth") * width
    kernel_grad = summed * (1.0 / math.sqrt(cells))
    return (output, input_grad, kernel_grad)


def solution(mesh):
    return jax.shard_map(
        per_device,
        mesh=mesh,
        in_specs=(
            P(None, "cin", "depth", None),
            P(None, "cout", "cin"),
            P("cin", "cout", "depth", None),
        ),
        out_specs=(
            P("cin", "cout", "depth", None),
            P("cout", "cin", "depth", None),
            P(None, "cout", "cin"),
        ),
        check_vma=False,
    )
```

profile of v0, /device:TPU:0, one launch (start us, length us, event | category | flops | bytes accessed | tf_op | source)
XLA Modules:
  0.0 189.4 jit_solution(8112478354780090528)
XLA Ops:
  7.2 1.0 copy.40
  8.2 2.4 %collective-permute-start = (bf16[8,64,1,128]{3,1,2,0:T(8,128)(2,1)S(1)}, bf16[8,64,1,128]{3,1,2,0:T(8,128)(2,1)S(1)}, u32[]{:S(2)}, u32[]{:S(2)}) collective-permute-start(bf16[8,64,1,128]{3,1,2,0:T(8,128)(2,1)S(1)} %get-tuple-element.25), channel_id=1, source_target_pairs={{0,1},{2,3},{4,5},{6,7},{8,9},{10,11},{12,13},{14,15},{16,17},{18,... | collective-permute-start | bytes 393224 | tf_op jit(solution)/shard_map/ppermute | solution.py:15
  10.6 1.3 collective-permute-start.1
  11.9 1.6 copy.55
  13.9 0.5 select_maximum_fusion
  14.4 0.7 fusion.85
  15.1 0.8 fusion.95
  15.9 0.9 fusion.94
  16.8 0.9 fusion.93
  17.6 0.8 fusion.92
  18.4 0.9 fusion.84
  19.3 1.0 fusion.83
  20.3 0.9 fusion.82
  21.2 0.8 fusion.91
  22.0 0.8 bitcast_dynamic-update-slice_fusion
  22.8 0.9 fusion.81
  23.7 0.7 fusion.73
  24.4 0.9 fusion.89
  25.2 0.8 fusion.88
  26.0 0.8 fusion.87
  26.9 0.9 fusion.80
  27.8 0.9 fusion.79
  28.7 28.0 %all-gather.2.cloned.1.call-done = bf16[8,256,2,128]{3,1,2,0:T(8,128)(2,1)} async-done(((bf16[1,256,2,128]{3,1,2,0:T(8,128)(2,1)}), bf16[8,256,2,128]{3,1,2,0:T(8,128)(2,1)}) %all-gather.2.cloned.1.call-update) | async-done | bytes 1048592 | tf_op jit(solution)/shard_map/all_gather | solution.py:80
  56.7 1.4 fusion.104
  58.0 1.3 collective-permute-start.2
  59.4 1.3 collective-permute-start.3
  60.7 0.9 fusion.86
  61.6 1.0 fusion.78
  62.6 0.8 fusion.68
  63.8 0.8 copy-done.1
  64.6 0.9 convolution_bitcast_fusion.1
  65.5 0.9 convolution_bitcast_fusion.2
  66.5 0.9 convolution_bitcast_fusion
  67.4 3.3 %fusion.54 = f32[8,64,2,128]{3,1,2,0:T(8,128)} fusion(f32[9,10,64,2,128]{4,2,3,1,0:T(8,128)S(1)} %convolution_bitcast_fusion, f32[9,10,64,2,128]{4,2,3,1,0:T(8,128)S(1)} %convolution_bitcast_fusion.1, f32[9,10,64,2,128]{4,2,0,3,1:T(8,128)S(1)} %convolution_bitcast_fusion.2), kind=kLoop, calls=%fused_computation.90 | loop fusion | flops 3407872 | bytes 22937600 | tf_op jit(solution)/shard_map/add | solution.py:98
  70.8 2.5 %convolution_bitcast_fusion.3 = f32[9,256,64]{1,2,0:T(8,128)S(1)} fusion(bf16[8,9,64,2,128]{4,2,3,0,1:T(8,128)(2,1)} %fusion.68, bf16[8,256,2,128]{3,1,2,0:T(8,128)(2,1)S(1)} %copy-done), kind=kOutput, calls=%fused_computation.55 | convolution fusion | flops 603979776 | bytes 3997696 | tf_op jit(solution)/shard_map/hodw,htcdw->toc/dot_general | solution.py:60
  73.3 2.5 %convolution_bitcast_fusion.4 = f32[9,256,64]{1,2,0:T(8,128)S(1)} fusion(bf16[8,9,64,2,128]{4,2,3,0,1:T(8,128)(2,1)} %get-tuple-element.9, bf16[8,256,2,128]{3,1,2,0:T(8,128)(2,1)S(1)} %copy-done), kind=kOutput, calls=%fused_computation.56 | convolution fusion | flops 603979776 | bytes 3997696 | tf_op jit(solution)/shard_map/hodw,htcdw->toc/dot_general | solution.py:60
  75.8 2.6 %fusion.19 = f32[9,256,64]{1,2,0:T(8,128)S(1)} fusion(bf16[8,9,64,2,128]{4,2,1,3,0:T(8,128)(2,1)} %fusion.86, bf16[8,256,2,128]{3,1,2,0:T(8,128)(2,1)S(1)} %copy-done), kind=kOutput, calls=%fused_computation.54 | convolution fusion | flops 603979776 | bytes 3997696 | tf_op jit(solution)/shard_map/hodw,htcdw->toc/dot_general | solution.py:60
  78.3 1.4 pad_maximum_fusion
  80.0 2.7 %fusion.13 = f32[8,2,128,256,1]{3,2,0,1,4:T(8,128)S(1)} fusion(bf16[8,9,64,2,128]{4,2,3,0,1:T(8,128)(2,1)} %get-tuple-element.9, bf16[27,256,64]{1,2,0:T(8,128)(2,1)S(1)} %copy-done.1), kind=kOutput, calls=%fused_computation.40 | convolution fusion | flops 603979776 | bytes 4751360 | tf_op jit(solution)/shard_map/toc,htcdw->hodw/dot_general | solution.py:35
  82.7 2.7 %fusion.11 = f32[8,2,128,256,1]{3,2,0,1,4:T(8,128)S(1)} fusion(bf16[8,9,64,2,128]{4,2,3,0,1:T(8,128)(2,1)} %fusion.68, bf16[27,256,64]{1,2,0:T(8,128)(2,1)S(1)} %copy-done.1), kind=kOutput, calls=%fused_computation.38 | convolution fusion | flops 603979776 | bytes 4751360 | tf_op jit(solution)/shard_map/toc,htcdw->hodw/dot_general | solution.py:35
  85.5 4.1 %fusion.15 = f32[8,256,2,128]{1,3,2,0:T(8,128)} fusion(f32[8,2,128,256,1]{3,2,0,1,4:T(8,128)S(1)} %fusion.11, f32[8,2,128,256,1]{3,2,0,1,4:T(8,128)S(1)} %fusion.13, bf16[8,9,64,2,128]{4,2,1,3,0:T(8,128)(2,1)} %fusion.86, bf16[27,256,64]{1,2,0:T(8,128)(2,1)S(1)} %copy-done.1), kind=kOutput, calls=%fused_computation.43 | convolution fusion | flops 605028352 | bytes 8945664 | tf_op jit(solution)/shard_map/toc,htcdw->hodw/dot_general | solution.py:35
  89.6 1.0 convert_element_type.15
  90.6 0.8 copy.73
  91.4 17.4 %all-reduce.7.cloned.1.call-done = f32[27,256,64]{1,2,0:T(8,128)} async-done(((f32[27,256,64]{1,2,0:T(8,128)}), f32[27,256,64]{1,2,0:T(8,128)}) %all-reduce.7.cloned.1.call-update) | async-done | bytes 1769488 | tf_op jit(solution)/shard_map/psum | solution.py:112
  108.8 2.9 %broadcast_multiply_fusion = f32[27,256,64]{1,2,0:T(8,128)} fusion(f32[27,256,64]{1,2,0:T(8,128)} %all-reduce.7.cloned.1.call-done), kind=kLoop, calls=%fused_computation.58 | loop fusion | flops 442368 | bytes 3538944 | tf_op jit(solution)/shard_map/mul | solution.py:114
  111.7 69.4 %reduce-scatter.3.cloned.1.call-done = f32[1,256,2,128]{1,3,2,0:T(8,128)} async-done(((f32[8,256,2,128]{1,3,2,0:T(8,128)}), f32[1,256,2,128]{1,3,2,0:T(8,128)}) %reduce-scatter.3.cloned.1.call-update) | async-done | bytes 262160 | tf_op jit(solution)/shard_map/reduce_scatter | solution.py:74
  181.1 1.0 convert_element_type.14
  182.1 0.8 copy.72
  (20 shorter events, 1.1 us)
Async XLA Ops:
  7.2 49.5 %all-gather.2.cloned.1.call-start = ((), (), s32[]{:S(2)}) async-start(), calls=%async_computation.3 | async-start | bytes 1179648 | tf_op jit(solution)/shard_map/all_gather | solution.py:80
  8.2 5.3 %collective-permute-start = (bf16[8,64,1,128]{3,1,2,0:T(8,128)(2,1)S(1)}, bf16[8,64,1,128]{3,1,2,0:T(8,128)(2,1)S(1)}, u32[]{:S(2)}, u32[]{:S(2)}) collective-permute-start(bf16[8,64,1,128]{3,1,2,0:T(8,128)(2,1)S(1)} %get-tuple-element.25), channel_id=1, source_target_pairs={{0,1},{2,3},{4,5},{6,7},{8,9},{10,11},{12,13},{14,15},{16,17},{18,... | collective-permute-start | bytes 393224 | tf_op jit(solution)/shard_map/ppermute | solution.py:15
  10.6 3.2 %collective-permute-start.1 = (bf16[8,64,1,128]{3,1,2,0:T(8,128)(2,1)S(1)}, bf16[8,64,1,128]{3,1,2,0:T(8,128)(2,1)S(1)}, u32[]{:S(2)}, u32[]{:S(2)}) collective-permute-start(bf16[8,64,1,128]{3,1,2,0:T(8,128)(2,1)S(1)} %get-tuple-element.26), channel_id=1, source_target_pairs={{1,0},{3,2},{5,4},{7,6},{9,8},{11,10},{13,12},{15,14},{17,16},{19,... | collective-permute-start | bytes 393224 | tf_op jit(solution)/shard_map/ppermute | solution.py:16
  13.5 76.1 %reduce-scatter.5.cloned.1.call-start = ((), (), s32[]{:S(2)}) async-start(), calls=%async_computation.4 | async-start | bytes 786432 | tf_op jit(solution)/shard_map/reduce_scatter | solution.py:107
  16.8 5.2 %copy-start.2 = (bf16[8,64,2,128]{3,2,1,0:T(2,128)(2,1)S(1)}, bf16[8,64,2,128]{3,2,1,0:T(2,128)(2,1)}, u32[]{:S(2)}) copy-start(bf16[8,64,2,128]{3,2,1,0:T(2,128)(2,1)} %param.3) | copy-start | bytes 786436
  56.7 6.8 %copy-start = (bf16[8,256,2,128]{3,1,2,0:T(8,128)(2,1)S(1)}, bf16[8,256,2,128]{3,1,2,0:T(8,128)(2,1)}, u32[]{:S(2)}) copy-start(bf16[8,256,2,128]{3,1,2,0:T(8,128)(2,1)} %all-gather.2.cloned.1.call-done) | copy-start | bytes 3145732
  58.0 5.4 %collective-permute-start.2 = (bf16[8,256,1,128]{3,1,2,0:T(8,128)(2,1)S(1)}, bf16[8,256,1,128]{3,1,2,0:T(8,128)(2,1)S(1)}, u32[]{:S(2)}, u32[]{:S(2)}) collective-permute-start(bf16[8,256,1,128]{3,1,2,0:T(8,128)(2,1)S(1)} %get-tuple-element.23), channel_id=1, source_target_pairs={{0,1},{2,3},{4,5},{6,7},{8,9},{10,11},{12,13},{14,15},{16,17},{18,... | collective-permute-start | bytes 1572872 | tf_op jit(solution)/shard_map/ppermute | solution.py:15
  59.4 4.1 %collective-permute-start.3 = (bf16[8,256,1,128]{3,1,2,0:T(8,128)(2,1)S(1)}, bf16[8,256,1,128]{3,1,2,0:T(8,128)(2,1)S(1)}, u32[]{:S(2)}, u32[]{:S(2)}) collective-permute-start(bf16[8,256,1,128]{3,1,2,0:T(8,128)(2,1)S(1)} %get-tuple-element.24), channel_id=1, source_target_pairs={{1,0},{3,2},{5,4},{7,6},{9,8},{11,10},{13,12},{15,14},{17,16},{19,... | collective-permute-start | bytes 1572872 | tf_op jit(solution)/shard_map/ppermute | solution.py:16
  63.4 1.2 copy-start.1
  70.8 38.1 %all-reduce.7.cloned.1.call-start = ((), (), s32[]{:S(2)}) async-start(), calls=%async_computation.5 | async-start | bytes 3538944 | tf_op jit(solution)/shard_map/psum | solution.py:112
  79.7 101.4 %reduce-scatter.3.cloned.1.call-start = ((), (), s32[]{:S(2)}) async-start(), calls=%async_computation.2 | async-start | bytes 2359296 | tf_op jit(solution)/shard_map/reduce_scatter | solution.py:74
Sparse Core Ops, SparseCore 0:
  13.6 42.9 all-gather.1
  70.9 14.0 reduce-scatter.4
  88.1 20.6 all-reduce.6
  112.2 68.8 reduce-scatter.2
where the time goes:
time: 190 us; the launch traced here: 189 us
  waiting for transfers between devices  115 us (61%)
  local copies, waits for them, and re-layouts  21.9 us (12%)
  matrix products  19.9 us (10%)
  between operations  13.9 us (7%)
  other arithmetic  11.9 us (6%)
  starting transfers between devices  6.61 us (3%)
    reduce_scatter x1, waiting for transfers between devices, per_device(): lax.psum_scatter(conv_rows(block, kernel, lax.axis_size('cin') * rows_own...  69.4 us
    all_gather x1, waiting for transfers between devices, per_device(): grad_full = lax.all_gather(grad_out, 'cin', axis=0, tiled=True)  28 us
    unnamed x25, local copies, waits for them, and re-layouts  17.7 us
    psum x1, waiting for transfers between devices, per_device(): summed = lax.psum(local_terms, 'depth')  17.4 us
    dot_general x3, matrix products, conv_rows(): jnp.einsum('toc,htcdw->hodw', weight[9 * depth_off:9 * depth_off + 9], st...  9.56 us
    dot_general x3, matrix products, weight_terms(): jnp.einsum('hodw,htcdw->toc', grad_own, stacked, preferred_element_type=j...  7.5 us
  transfers between devices with their start and end apart: 8, of which 4 were waited for; matrix products, arithmetic and copies ran while one was open for 22% of the time, Pallas kernels for 0%

commit v1 on v0

--- a/solution.py
+++ b/solution.py
@@ -77,7 +77,12 @@
         scatter_dimension=0,
         tiled=True,
     ).astype(jnp.bfloat16)
-    grad_full = lax.all_gather(grad_out, "cin", axis=0, tiled=True)
+    ring = [grad_out]
+    for hop in range(7):
+        ring.append(lax.ppermute(ring[-1], "cin", [(dev, (dev + 1) % 8) for dev in range(8)]))
+    grad_full = jnp.roll(
+        jnp.concatenate(ring[::-1], axis=0), (lax.axis_index("cin") + 1) * ring[0].shape[0], axis=0
+    )
     grad_full = padded_2(grad_full, (("depth", 2),), 1)
     grad_pad = jnp.pad(grad_full, ((1, 1), (0, 0), (0, 0), (0, 0)))
     rows_grad = rows_all // lax.axis_size("cout")

time: 190 us -> 176 us (0.926)
  local copies, waits for them, and re-layouts: 21.9 us -> 11.5 us
  matrix products: 19.9 us -> 11.4 us
  starting transfers between devices: 6.61 us -> 8.96 us
  between operations: 13.9 us -> 16 us
  waiting for transfers between devices: 115 us -> 117 us
    ppermute x0 -> x7, waiting for transfers between devices: none -> 49.8 us  [per_device(): lax.ppermute(ring[-1], 'cin', [(dev, (dev + 1) % 8) for dev in range(8)])]
    all_gather x1 -> x0, waiting for transfers between devices: 28 us -> none  [per_device(): grad_full = lax.all_gather(grad_out, 'cin', axis=0, tiled=True)]
    reduce_scatter x1, waiting for transfers between devices: 69.4 us -> 57.4 us  [per_device(): lax.psum_scatter(conv_rows(block, kernel, lax.axis_size('cin') * rows_own...]
    psum x1, waiting for transfers between devices: 17.4 us -> 8.79 us  [per_device(): summed = lax.psum(local_terms, 'depth')]
    unnamed x25 -> x56, local copies, waits for them, and re-layouts: 17.7 us -> 10.4 us
    dot_general x3, matrix products: 7.5 us -> 2.42 us  [weight_terms(): jnp.einsum('hodw,htcdw->toc', grad_own, stacked, preferred_element_type=j...]
    dot_general x3, matrix products: 9.56 us -> 6.2 us  [conv_rows(): jnp.einsum('toc,htcdw->hodw', weight[9 * depth_off:9 * depth_off + 9], st...]
    ppermute x0 -> x7, starting transfers between devices: none -> 2.39 us  [per_device(): lax.ppermute(ring[-1], 'cin', [(dev, (dev + 1) % 8) for dev in range(8)])]
  transfers between devices with their start and end apart: 8 -> 14, of which waited for: 4 -> 10; matrix products, arithmetic and copies ran while one was open for 22% -> 11% of each run, Pallas kernels for 0% -> 0%
where the time goes in v1:
time: 176 us; the launch traced here: 175 us
  waiting for transfers between devices  117 us (66%)
  between operations  16 us (9%)
  local copies, waits for them, and re-layouts  11.5 us (7%)
  matrix products  11.4 us (6%)
  other arithmetic  10.4 us (6%)
  starting transfers between devices  8.96 us (5%)
    reduce_scatter x1, waiting for transfers between devices, per_device(): lax.psum_scatter(conv_rows(block, kernel, lax.axis_size('cin') * rows_own...  57.4 us
    ppermute x7, waiting for transfers between devices, per_device(): lax.ppermute(ring[-1], 'cin', [(dev, (dev + 1) % 8) for dev in range(8)])  49.8 us
    unnamed x56, local copies, waits for them, and re-layouts  10.4 us
    psum x1, waiting for transfers between devices, per_device(): summed = lax.psum(local_terms, 'depth')  8.79 us
    dot_general x3, matrix products, conv_rows(): jnp.einsum('toc,htcdw->hodw', weight[9 * depth_off:9 * depth_off + 9], st...  6.2 us
    ppermute x2, starting transfers between devices, padded_2(): before = lax.ppermute(last, axis, up)  3.69 us
  transfers between devices with their start and end apart: 14, of which 10 were waited for; matrix products, arithmetic and copies ran while one was open for 11% of the time, Pallas kernels for 0%

profile of v1, /device:TPU:0, one launch (start us, length us, event | category | flops | bytes accessed | tf_op | source)
XLA Modules:
  0.0 175.1 jit_solution(4281684894889445763)
XLA Ops:
  8.0 1.0 copy.6
  9.1 2.4 %collective-permute-start = (bf16[8,64,1,128]{3,1,2,0:T(8,128)(2,1)S(1)}, bf16[8,64,1,128]{3,1,2,0:T(8,128)(2,1)S(1)}, u32[]{:S(2)}, u32[]{:S(2)}) collective-permute-start(bf16[8,64,1,128]{3,1,2,0:T(8,128)(2,1)S(1)} %get-tuple-element.22), channel_id=1, source_target_pairs={{0,1},{2,3},{4,5},{6,7},{8,9},{10,11},{12,13},{14,15},{16,17},{18,... | collective-permute-start | bytes 393224 | tf_op jit(solution)/shard_map/ppermute | solution.py:15
  11.4 1.3 collective-permute-start.1
  12.7 0.9 copy.21
  13.7 2.4 %collective-permute-start.2 = (bf16[1,256,2,128]{3,1,2,0:T(8,128)(2,1)S(1)}, bf16[1,256,2,128]{3,1,2,0:T(8,128)(2,1)S(1)}, u32[]{:S(2)}, u32[]{:S(2)}) collective-permute-start(bf16[1,256,2,128]{3,1,2,0:T(8,128)(2,1)S(1)} %copy.21), channel_id=1, source_target_pairs={{0,4},{4,8},{8,12},{12,16},{16,20},{20,24},{24,28},{28,0},{1,5},{5... | collective-permute-start | bytes 393224 | tf_op jit(solution)/shard_map/ppermute | solution.py:82
  16.1 0.5 select_maximum_fusion
  16.7 0.2 fusion.84
  16.9 0.4 fusion.83
  17.3 0.3 fusion.82
  17.6 0.2 fusion.81
  17.9 0.2 fusion.80
  18.2 0.2 fusion.79
  18.4 0.4 fusion.78
  18.9 4.2 %collective-permute-done.2 = bf16[1,256,2,128]{3,1,2,0:T(8,128)(2,1)S(1)} collective-permute-done((bf16[1,256,2,128]{3,1,2,0:T(8,128)(2,1)S(1)}, bf16[1,256,2,128]{3,1,2,0:T(8,128)(2,1)S(1)}, u32[]{:S(2)}, u32[]{:S(2)}) %collective-permute-start.2) | collective-permute-done | bytes 131104 | tf_op jit(solution)/shard_map/ppermute | solution.py:82
  23.3 8.1 %collective-permute-done.3 = bf16[1,256,2,128]{3,1,2,0:T(8,128)(2,1)S(1)} collective-permute-done((bf16[1,256,2,128]{3,1,2,0:T(8,128)(2,1)S(1)}, bf16[1,256,2,128]{3,1,2,0:T(8,128)(2,1)S(1)}, u32[]{:S(2)}, u32[]{:S(2)}) %collective-permute-start.3) | collective-permute-done | bytes 131104 | tf_op jit(solution)/shard_map/ppermute | solution.py:82
  31.6 7.5 %collective-permute-done.4 = bf16[1,256,2,128]{3,1,2,0:T(8,128)(2,1)S(1)} collective-permute-done((bf16[1,256,2,128]{3,1,2,0:T(8,128)(2,1)S(1)}, bf16[1,256,2,128]{3,1,2,0:T(8,128)(2,1)S(1)}, u32[]{:S(2)}, u32[]{:S(2)}) %collective-permute-start.4) | collective-permute-done | bytes 131104 | tf_op jit(solution)/shard_map/ppermute | solution.py:82
  39.1 7.5 %collective-permute-done.5 = bf16[1,256,2,128]{3,1,2,0:T(8,128)(2,1)S(1)} collective-permute-done((bf16[1,256,2,128]{3,1,2,0:T(8,128)(2,1)S(1)}, bf16[1,256,2,128]{3,1,2,0:T(8,128)(2,1)S(1)}, u32[]{:S(2)}, u32[]{:S(2)}) %collective-permute-start.5) | collective-permute-done | bytes 131104 | tf_op jit(solution)/shard_map/ppermute | solution.py:82
  46.9 7.5 %collective-permute-done.6 = bf16[1,256,2,128]{3,1,2,0:T(8,128)(2,1)S(1)} collective-permute-done((bf16[1,256,2,128]{3,1,2,0:T(8,128)(2,1)S(1)}, bf16[1,256,2,128]{3,1,2,0:T(8,128)(2,1)S(1)}, u32[]{:S(2)}, u32[]{:S(2)}) %collective-permute-start.6) | collective-permute-done | bytes 131104 | tf_op jit(solution)/shard_map/ppermute | solution.py:82
  54.4 7.6 %collective-permute-done.7 = bf16[1,256,2,128]{3,1,2,0:T(8,128)(2,1)S(1)} collective-permute-done((bf16[1,256,2,128]{3,1,2,0:T(8,128)(2,1)S(1)}, bf16[1,256,2,128]{3,1,2,0:T(8,128)(2,1)S(1)}, u32[]{:S(2)}, u32[]{:S(2)}) %collective-permute-start.7) | collective-permute-done | bytes 131104 | tf_op jit(solution)/shard_map/ppermute | solution.py:82
  62.2 7.5 %collective-permute-done.8 = bf16[1,256,2,128]{3,1,2,0:T(8,128)(2,1)S(1)} collective-permute-done((bf16[1,256,2,128]{3,1,2,0:T(8,128)(2,1)S(1)}, bf16[1,256,2,128]{3,1,2,0:T(8,128)(2,1)S(1)}, u32[]{:S(2)}, u32[]{:S(2)}) %collective-permute-start.8) | collective-permute-done | bytes 131104 | tf_op jit(solution)/shard_map/ppermute | solution.py:82
  70.3 1.3 collective-permute-start.9
  71.6 1.3 collective-permute-start.10
  73.1 0.2 fusion.68
  73.4 1.1 copy-done.2
  74.5 0.9 collective-permute-done.10
  75.4 0.3 fusion.5
  75.7 0.9 convolution_bitcast_fusion.1
  76.7 0.9 convolution_bitcast_fusion.2
  77.6 0.9 convolution_bitcast_fusion
  78.6 3.3 %fusion.54 = f32[8,64,2,128]{3,1,2,0:T(8,128)} fusion(f32[9,10,64,2,128]{4,2,3,1,0:T(8,128)S(1)} %convolution_bitcast_fusion, f32[9,10,64,2,128]{4,2,3,1,0:T(8,128)S(1)} %convolution_bitcast_fusion.1, f32[9,10,64,2,128]{4,2,0,3,1:T(8,128)S(1)} %convolution_bitcast_fusion.2), kind=kLoop, calls=%fused_computation.90 | loop fusion | flops 3407872 | bytes 22937600 | tf_op jit(solution)/shard_map/add | solution.py:103
  81.9 0.2 all-reduce.7.cloned.1.call-start
  82.1 0.8 convolution_bitcast_fusion.3
  82.9 0.8 copy-done.1
  83.8 0.8 convolution_bitcast_fusion.4
  84.8 0.6 copy-done.8
  85.4 0.8 fusion.19
  86.2 1.4 pad_maximum_fusion
  87.7 2.7 %fusion.13 = f32[8,2,128,256,1]{3,2,0,1,4:T(8,128)S(1)} fusion(bf16[8,9,64,2,128]{4,2,3,0,1:T(8,128)(2,1)} %copy-done, bf16[27,256,64]{1,2,0:T(8,128)(2,1)S(1)} %copy-done.6), kind=kOutput, calls=%fused_computation.40 | convolution fusion | flops 603979776 | bytes 4751360 | tf_op jit(solution)/shard_map/toc,htcdw->hodw/dot_general | solution.py:35
  90.4 1.0 fusion.11
  91.5 1.2 copy-done.4
  92.7 2.4 %fusion.15 = f32[8,256,2,128]{1,3,2,0:T(8,128)} fusion(f32[8,2,128,256,1]{3,2,0,1,4:T(8,128)S(1)} %fusion.11, f32[8,2,128,256,1]{3,2,0,1,4:T(8,128)S(1)} %fusion.13, bf16[8,9,64,2,128]{4,2,1,3,0:T(8,128)(2,1)S(1)} %copy-done.4, bf16[27,256,64]{1,2,0:T(8,128)(2,1)S(1)} %copy-done.6), kind=kOutput, calls=%fused_computation.43 | convolution fusion | flops 605028352 | bytes 8945664 | tf_op jit(solution)/shard_map/toc,htcdw->hodw/dot_general | solution.py:35
  95.2 1.0 convert_element_type.15
  96.1 0.8 copy.41
  96.9 8.8 %all-reduce.7.cloned.1.call-done = f32[27,256,64]{1,2,0:T(8,128)} async-done(((f32[27,256,64]{1,2,0:T(8,128)}), f32[27,256,64]{1,2,0:T(8,128)}) %all-reduce.7.cloned.1.call-update) | async-done | bytes 1769488 | tf_op jit(solution)/shard_map/psum | solution.py:117
  105.7 2.9 %broadcast_multiply_fusion = f32[27,256,64]{1,2,0:T(8,128)} fusion(f32[27,256,64]{1,2,0:T(8,128)} %all-reduce.7.cloned.1.call-done), kind=kLoop, calls=%fused_computation.58 | loop fusion | flops 442368 | bytes 3538944 | tf_op jit(solution)/shard_map/mul | solution.py:119
  108.6 57.4 %reduce-scatter.3.cloned.1.call-done = f32[1,256,2,128]{1,3,2,0:T(8,128)} async-done(((f32[8,256,2,128]{1,3,2,0:T(8,128)}), f32[1,256,2,128]{1,3,2,0:T(8,128)}) %reduce-scatter.3.cloned.1.call-update) | async-done | bytes 262160 | tf_op jit(solution)/shard_map/reduce_scatter | solution.py:74
  165.9 1.0 convert_element_type.14
  166.9 0.8 copy.40
  (64 shorter events, 2.3 us)
Async XLA Ops:
  8.0 87.1 %reduce-scatter.5.cloned.1.call-start = ((), (), s32[]{:S(2)}) async-start(), calls=%async_computation.3 | async-start | bytes 786432 | tf_op jit(solution)/shard_map/reduce_scatter | solution.py:112
  9.1 7.0 %collective-permute-start = (bf16[8,64,1,128]{3,1,2,0:T(8,128)(2,1)S(1)}, bf16[8,64,1,128]{3,1,2,0:T(8,128)(2,1)S(1)}, u32[]{:S(2)}, u32[]{:S(2)}) collective-permute-start(bf16[8,64,1,128]{3,1,2,0:T(8,128)(2,1)S(1)} %get-tuple-element.22), channel_id=1, source_target_pairs={{0,1},{2,3},{4,5},{6,7},{8,9},{10,11},{12,13},{14,15},{16,17},{18,... | collective-permute-start | bytes 393224 | tf_op jit(solution)/shard_map/ppermute | solution.py:15
  11.4 4.6 %collective-permute-start.1 = (bf16[8,64,1,128]{3,1,2,0:T(8,128)(2,1)S(1)}, bf16[8,64,1,128]{3,1,2,0:T(8,128)(2,1)S(1)}, u32[]{:S(2)}, u32[]{:S(2)}) collective-permute-start(bf16[8,64,1,128]{3,1,2,0:T(8,128)(2,1)S(1)} %get-tuple-element.23), channel_id=1, source_target_pairs={{1,0},{3,2},{5,4},{7,6},{9,8},{11,10},{13,12},{15,14},{17,16},{19,... | collective-permute-start | bytes 393224 | tf_op jit(solution)/shard_map/ppermute | solution.py:16
  13.7 9.4 %collective-permute-start.2 = (bf16[1,256,2,128]{3,1,2,0:T(8,128)(2,1)S(1)}, bf16[1,256,2,128]{3,1,2,0:T(8,128)(2,1)S(1)}, u32[]{:S(2)}, u32[]{:S(2)}) collective-permute-start(bf16[1,256,2,128]{3,1,2,0:T(8,128)(2,1)S(1)} %copy.21), channel_id=1, source_target_pairs={{0,4},{4,8},{8,12},{12,16},{16,20},{20,24},{24,28},{28,0},{1,5},{5... | collective-permute-start | bytes 393224 | tf_op jit(solution)/shard_map/ppermute | solution.py:82
  16.0 1.5 copy-start.10
  18.9 50.9 %copy-start = (bf16[8,9,64,2,128]{4,2,3,0,1:T(8,128)(2,1)}, bf16[8,9,64,2,128]{4,2,3,0,1:T(8,128)(2,1)S(1)}, u32[]{:S(2)}) copy-start(bf16[8,9,64,2,128]{4,2,3,0,1:T(8,128)(2,1)S(1)} %get-tuple-element.8) | copy-start | bytes 7077892
  23.1 8.3 %collective-permute-start.3 = (bf16[1,256,2,128]{3,1,2,0:T(8,128)(2,1)S(1)}, bf16[1,256,2,128]{3,1,2,0:T(8,128)(2,1)S(1)}, u32[]{:S(2)}, u32[]{:S(2)}) collective-permute-start(bf16[1,256,2,128]{3,1,2,0:T(8,128)(2,1)S(1)} %collective-permute-done.2), channel_id=1, source_target_pairs={{0,4},{4,8},{8,12},{12,16},{16,20},{20,24},{24,28},{28,0},{1,5},{5... | collective-permute-start | bytes 393224 | tf_op jit(solution)/shard_map/ppermute | solution.py:82
  31.4 7.7 %collective-permute-start.4 = (bf16[1,256,2,128]{3,1,2,0:T(8,128)(2,1)S(1)}, bf16[1,256,2,128]{3,1,2,0:T(8,128)(2,1)S(1)}, u32[]{:S(2)}, u32[]{:S(2)}) collective-permute-start(bf16[1,256,2,128]{3,1,2,0:T(8,128)(2,1)S(1)} %collective-permute-done.3), channel_id=1, source_target_pairs={{0,4},{4,8},{8,12},{12,16},{16,20},{20,24},{24,28},{28,0},{1,5},{5... | collective-permute-start | bytes 393224 | tf_op jit(solution)/shard_map/ppermute | solution.py:82
  31.6 38.3 %copy-start.9 = (bf16[1,256,2,128]{3,2,1,0:T(2,128)(2,1)S(1)}, bf16[1,256,2,128]{3,2,1,0:T(2,128)(2,1)}, u32[]{:S(2)}) copy-start(bf16[1,256,2,128]{3,2,1,0:T(2,128)(2,1)} %param.5) | copy-start | bytes 393220
  39.0 7.7 %collective-permute-start.5 = (bf16[1,256,2,128]{3,1,2,0:T(8,128)(2,1)S(1)}, bf16[1,256,2,128]{3,1,2,0:T(8,128)(2,1)S(1)}, u32[]{:S(2)}, u32[]{:S(2)}) collective-permute-start(bf16[1,256,2,128]{3,1,2,0:T(8,128)(2,1)S(1)} %collective-permute-done.4), channel_id=1, source_target_pairs={{0,4},{4,8},{8,12},{12,16},{16,20},{20,24},{24,28},{28,0},{1,5},{5... | collective-permute-start | bytes 393224 | tf_op jit(solution)/shard_map/ppermute | solution.py:82
  46.7 7.7 %collective-permute-start.6 = (bf16[1,256,2,128]{3,1,2,0:T(8,128)(2,1)S(1)}, bf16[1,256,2,128]{3,1,2,0:T(8,128)(2,1)S(1)}, u32[]{:S(2)}, u32[]{:S(2)}) collective-permute-start(bf16[1,256,2,128]{3,1,2,0:T(8,128)(2,1)S(1)} %collective-permute-done.5), channel_id=1, source_target_pairs={{0,4},{4,8},{8,12},{12,16},{16,20},{20,24},{24,28},{28,0},{1,5},{5... | collective-permute-start | bytes 393224 | tf_op jit(solution)/shard_map/ppermute | solution.py:82
  54.4 7.7 %collective-permute-start.7 = (bf16[1,256,2,128]{3,1,2,0:T(8,128)(2,1)S(1)}, bf16[1,256,2,128]{3,1,2,0:T(8,128)(2,1)S(1)}, u32[]{:S(2)}, u32[]{:S(2)}) collective-permute-start(bf16[1,256,2,128]{3,1,2,0:T(8,128)(2,1)S(1)} %collective-permute-done.6), channel_id=1, source_target_pairs={{0,4},{4,8},{8,12},{12,16},{16,20},{20,24},{24,28},{28,0},{1,5},{5... | collective-permute-start | bytes 393224 | tf_op jit(solution)/shard_map/ppermute | solution.py:82
  62.0 7.7 %collective-permute-start.8 = (bf16[1,256,2,128]{3,1,2,0:T(8,128)(2,1)S(1)}, bf16[1,256,2,128]{3,1,2,0:T(8,128)(2,1)S(1)}, u32[]{:S(2)}, u32[]{:S(2)}) collective-permute-start(bf16[1,256,2,128]{3,1,2,0:T(8,128)(2,1)S(1)} %collective-permute-done.7), channel_id=1, source_target_pairs={{0,4},{4,8},{8,12},{12,16},{16,20},{20,24},{24,28},{28,0},{1,5},{5... | collective-permute-start | bytes 393224 | tf_op jit(solution)/shard_map/ppermute | solution.py:82
  70.2 3.2 %copy-start.7 = (bf16[16,256,2,128]{3,1,2,0:T(8,128)(2,1)}, bf16[16,256,2,128]{3,1,2,0:T(8,128)(2,1)S(1)}, u32[]{:S(2)}) copy-start(bf16[16,256,2,128]{3,1,2,0:T(8,128)(2,1)S(1)} %constant_dynamic-update-slice_fusion) | copy-start | bytes 6291460
  70.3 3.2 %collective-permute-start.9 = (bf16[8,256,1,128]{3,1,2,0:T(8,128)(2,1)S(1)}, bf16[8,256,1,128]{3,1,2,0:T(8,128)(2,1)S(1)}, u32[]{:S(2)}, u32[]{:S(2)}) collective-permute-start(bf16[8,256,1,128]{3,1,2,0:T(8,128)(2,1)S(1)} %get-tuple-element.6), channel_id=1, source_target_pairs={{0,1},{2,3},{4,5},{6,7},{8,9},{10,11},{12,13},{14,15},{16,17},{18,... | collective-permute-start | bytes 1572872 | tf_op jit(solution)/shard_map/ppermute | solution.py:15
  71.6 3.8 %collective-permute-start.10 = (bf16[8,256,1,128]{3,1,2,0:T(8,128)(2,1)S(1)}, bf16[8,256,1,128]{3,1,2,0:T(8,128)(2,1)S(1)}, u32[]{:S(2)}, u32[]{:S(2)}) collective-permute-start(bf16[8,256,1,128]{3,1,2,0:T(8,128)(2,1)S(1)} %get-tuple-element.7), channel_id=1, source_target_pairs={{1,0},{3,2},{5,4},{7,6},{9,8},{11,10},{13,12},{15,14},{17,16},{19,... | collective-permute-start | bytes 1572872 | tf_op jit(solution)/shard_map/ppermute | solution.py:16
  73.1 1.5 copy-start.2
  73.4 2.3 %copy-start.5 = (bf16[27,256,64]{1,2,0:T(8,128)(2,1)S(1)}, bf16[27,256,64]{1,2,0:T(8,128)(2,1)}, u32[]{:S(2)}) copy-start(bf16[27,256,64]{1,2,0:T(8,128)(2,1)} %param.4) | copy-start | bytes 2654212
  81.9 23.8 %all-reduce.7.cloned.1.call-start = ((), (), s32[]{:S(2)}) async-start(), calls=%async_computation.4 | async-start | bytes 3538944 | tf_op jit(solution)/shard_map/psum | solution.py:117
  82.1 1.7 copy-start.1
  82.9 1.8 %copy-start.3 = (bf16[8,9,64,2,128]{4,2,1,3,0:T(8,128)(2,1)S(1)}, bf16[8,9,64,2,128]{4,2,1,3,0:T(8,128)(2,1)}, u32[]{:S(2)}) copy-start(bf16[8,9,64,2,128]{4,2,1,3,0:T(8,128)(2,1)} %copy-done.2) | copy-start | bytes 7077892
  82.9 2.5 %copy-start.8 = (bf16[16,256,2,128]{3,1,2,0:T(8,128)(2,1)S(1)}, bf16[16,256,2,128]{3,1,2,0:T(8,128)(2,1)}, u32[]{:S(2)}) copy-start(bf16[16,256,2,128]{3,1,2,0:T(8,128)(2,1)} %copy-done.7) | copy-start | bytes 6291460
  86.2 1.5 copy-start.6
  87.6 78.3 %reduce-scatter.3.cloned.1.call-start = ((), (), s32[]{:S(2)}) async-start(), calls=%async_computation.2 | async-start | bytes 2359296 | tf_op jit(solution)/shard_map/reduce_scatter | solution.py:74
  90.4 2.2 %copy-start.4 = (bf16[8,9,64,2,128]{4,2,1,3,0:T(8,128)(2,1)S(1)}, bf16[8,9,64,2,128]{4,2,1,3,0:T(8,128)(2,1)}, u32[]{:S(2)}) copy-start(bf16[8,9,64,2,128]{4,2,1,3,0:T(8,128)(2,1)} %copy-done.2) | copy-start | bytes 7077892
Sparse Core Ops, SparseCore 0:
  82.0 12.2 reduce-scatter.4
  98.2 67.6 reduce-scatter.2
Sparse Core Ops, SparseCore 1:
  87.7 17.9 all-reduce.6
